TPU v7x, 768 devices: a whole 4x8x12 slice. The times are simulated.
768 devices in a mesh: loop: 96 (over y, x, z_lo), rep: 8 (over z_hi, core).
Axes of the slice: x: 4, y: 8, z: 12 (z_hi: 4, z_lo: 3; z = z_hi * 3 + z_lo), core: 2. Of those that a mesh axis runs over, the one named last changes fastest.
Arguments:
- features: bfloat16 [98304, 256], P(('loop', 'rep')), may hold values from -6 to 6
- kernel_tiles: bfloat16 [768, 128, 128, 128], P(('loop', 'rep')), may hold values from -0.125 to 0.125
- row_starts: int32 [768, 9], P(('loop', 'rep')), may hold values from 0 to 128, as said below
- column_block: int32 [768, 128], P(('loop', 'rep')), may hold values from 0 to 767, as said below
- self_weight: bfloat16 [256, 256], replicated, may hold values from -0.375 to 0.375
- kernel_weight: bfloat16 [256, 256], replicated, may hold values from -0.375 to 0.375
- cotangent: bfloat16 [98304, 256], P(('loop', 'rep')), may hold values from -28 to 28
Outputs:
- layer_out: bfloat16 [98304, 256], P(('loop', 'rep'))
- feature_grad: bfloat16 [98304, 256], P(('loop', 'rep'))
- weight_grads: float32 [2, 256, 256], replicated
Inputs may be any that keep to these rules, and one draw needn't show every extreme that they name: `row_starts`: in each row, the entries start at 0 and never fall; the last is the group's live slot count, at least 32, and some group has 128 live slots. column_block[d, s] // 8 differs from d // 8 by at most 1; the live slots of one group hold distinct pairs of row block and column block.
All inputs are finite; a program needn't handle non-finite values.
Results may differ from a plain program's by a relative error of at most 0.025.
Values may be sent and summed in bfloat16 or wider, within the bound.
A program may use at most 64 MiB of HBM per device.

v0:
```python
import math

import jax
import jax.numpy as jnp
from jax import lax
from jax.sharding import PartitionSpec as P

REACH = 1


def from_behind(value, axis, steps):
    count = lax.axis_size(axis)
    leading, last = (max(0, -steps), min(count, count - steps))
    return lax.ppermute(value, axis, [(source, source + steps) for source in range(leading, last)])


def slot_rows(row_starts, slot_count, stripes):
    slot_ids = jnp.arange(slot_count, dtype=jnp.int32)
    interior = row_starts[0, 1:stripes]
    row_of = jnp.sum((interior[None, :] <= slot_ids[:, None]).astype(jnp.int32), axis=1)
    live_flag = (slot_ids < row_starts[0, stripes]).astype(jnp.int32)
    return (row_of, live_flag)


def on_device(
    features, kernel_tiles, row_starts, column_block, self_weight, kernel_weight, cotangent
):
    stripes = lax.axis_size("rep")
    bands = lax.axis_size("loop")
    tile_edge = features.shape[0]
    channels = features.shape[1]
    slot_count = kernel_tiles.shape[1]
    tiles_here = kernel_tiles[0]
    band = lax.axis_index("loop")
    span = 2 * REACH + 1
    across = span * stripes
    near = []
    for distance in range(-REACH, REACH + 1):
        if distance == 0:
            near.append(features)
        else:
            near.append(from_behind(features, "loop", -distance))
    band_stack = jnp.stack(near)[:, None]
    band_rows = lax.all_gather(band_stack, "rep", axis=1, tiled=True).reshape(
        across, tile_edge, channels
    )
    row_of, live_flag = slot_rows(row_starts, slot_count, stripes)
    col_local = column_block[0] - (band - REACH) * stripes
    live_mask = live_flag.astype(jnp.float32)
    offset_pick = col_local[:, None] == jnp.arange(across, dtype=jnp.int32)[None, :]
    row_pick = (row_of[:, None] == jnp.arange(stripes, dtype=jnp.int32)[None, :]).astype(
        jnp.float32
    )
    live_pick = row_pick * live_mask[:, None]
    target_pick = offset_pick.astype(jnp.float32) * live_mask[:, None]
    source_pick = offset_pick.astype(jnp.bfloat16)
    per_turn = 16
    turns = slot_count // per_turn

    def forward_turn(turn, running):
        offset = turn * per_turn
        sources = lax.dynamic_slice_in_dim(source_pick, offset, per_turn, 0)
        near_rows = jnp.einsum(
            "so,oaf->saf", sources, band_rows, preferred_element_type=jnp.float32
        ).astype(jnp.bfloat16)
        tile_block = lax.dynamic_slice_in_dim(tiles_here, offset, per_turn, 0)
        products = jnp.einsum(
            "sab,sbf->saf", tile_block, near_rows, preferred_element_type=jnp.float32
        )
        weights = lax.dynamic_slice_in_dim(live_pick, offset, per_turn, 0)
        return running + jnp.einsum("sr,saf->raf", weights, products)

    partial_rows = lax.fori_loop(
        0, turns, forward_turn, jnp.zeros((stripes, tile_edge, channels), jnp.float32)
    )
    partial_rows = partial_rows.reshape(stripes * tile_edge, channels)
    norm_scale = 1.0 / math.sqrt(tile_edge * bands * stripes)
    kernel_sum = lax.psum_scatter(partial_rows, "rep", scatter_dimension=0, tiled=True)
    kernel_rows = kernel_sum.astype(jnp.bfloat16)
    preact = jnp.dot(features, self_weight, preferred_element_type=jnp.float32) + jnp.dot(
        kernel_rows, kernel_weight, preferred_element_type=jnp.float32
    )
    activated, pullback = jax.vjp(jax.nn.gelu, preact)
    layer_out = activated.astype(jnp.bfloat16)
    grad_pre = pullback(cotangent.astype(jnp.float32))[0].astype(jnp.bfloat16)
    own_grad = jnp.dot(grad_pre, kernel_weight.T, preferred_element_type=jnp.float32).astype(
        jnp.bfloat16
    )
    kernel_grad = lax.all_gather(own_grad, "rep", axis=0, tiled=True)
    contract = (((0,), (0,)), ((), ()))
    grad_terms = jnp.stack(
        [
            lax.dot_general(features, grad_pre, contract, preferred_element_type=jnp.float32),
            lax.dot_general(kernel_rows, grad_pre, contract, preferred_element_type=jnp.float32),
        ]
    )
    weight_grads = lax.psum(grad_terms, ("loop", "rep")) * norm_scale
    grad_blocks = kernel_grad.reshape(stripes, tile_edge, channels)
    row_pick_half = row_pick.astype(jnp.bfloat16)

    def backward_turn(turn, running):
        offset = turn * per_turn
        rows_here = lax.dynamic_slice_in_dim(row_pick_half, offset, per_turn, 0)
        left_rows = jnp.einsum(
            "sr,raf->saf", rows_here, grad_blocks, preferred_element_type=jnp.float32
        ).astype(jnp.bfloat16)
        tile_block = lax.dynamic_slice_in_dim(tiles_here, offset, per_turn, 0)
        products = jnp.einsum(
            "sab,saf->sbf", tile_block, left_rows, preferred_element_type=jnp.float32
        )
        targets = lax.dynamic_slice_in_dim(target_pick, offset, per_turn, 0)
        return running + jnp.einsum("so,sbf->obf", targets, products)

    returned = lax.fori_loop(
        0, turns, backward_turn, jnp.zeros((across, tile_edge, channels), jnp.float32)
    )
    returned = lax.psum_scatter(
        returned.reshape(span, stripes, tile_edge, channels).astype(jnp.bfloat16),
        "rep",
        scatter_dimension=1,
        tiled=True,
    ).astype(jnp.float32)
    feature_sum = (
        jnp.dot(grad_pre, self_weight.T, preferred_element_type=jnp.float32) + returned[REACH, 0]
    )
    for distance in range(-REACH, REACH + 1):
        if distance != 0:
            feature_sum = feature_sum + from_behind(
                returned[distance + REACH, 0].astype(jnp.bfloat16), "loop", distance
            ).astype(jnp.float32)
    feature_grad = feature_sum.astype(jnp.bfloat16)
    return (layer_out, feature_grad, weight_grads)


def solution(mesh):
    placed = (
        P(("loop", "rep"), None),
        P(("loop", "rep"), None, None, None),
        P(("loop", "rep"), None),
        P(("loop", "rep"), None),
        P(),
        P(),
        P(("loop", "rep"), None),
    )
    return jax.shard_map(
        on_device,
        mesh=mesh,
        in_specs=placed,
        out_specs=(P(("loop", "rep"), None), P(("loop", "rep"), None), P()),
        check_vma=False,
    )
```

profile of v0, /device:TPU:1, one launch (start us, length us, event | category | flops | bytes accessed | tf_op | source)
XLA Modules:
  0.0 826.1 jit_solution(8199755593625965090)
XLA Ops:
  7.2 1.3 collective-permute-start.1
  8.5 5.5 collective-permute-start
  14.0 1.6 collective-permute-done
  15.6 1.5 pad_maximum_fusion.1
  17.2 1.2 slice.19
  20.7 60.3 %all-gather.3.cloned.1.call-done = bf16[3,1024,256]{2,1,0:T(8,128)(2,1)} async-done(((bf16[3,128,256]{2,1,0:T(8,128)(2,1)}), bf16[3,1024,256]{2,1,0:T(8,128)(2,1)}) %all-gather.3.cloned.1.call-update) | async-done | bytes 1572880 | tf_op jit(solution)/shard_map/all_gather | solution.py:44
  81.0 2.3 copy.48
  83.2 38.4 %while.28 = (s32[]{:T(128)}, f32[8,128,256]{2,0,1:T(8,128)}, bf16[128,8]{0,1:T(8,128)(2,1)S(1)}, bf16[128,128,128]{2,1,0:T(8,128)(2,1)}, bf16[128,24]{1,0:T(8,12...) while((s32[]{:T(128)}, f32[8,128,256]{2,0,1:T(8,128)}, ...), condition=%wide.region_2.0_spmd.clone, body=%wide.region_1.0_spmd.clone.sunk | while | flops 168820736 | bytes 8394929 | solution.py:73
  83.7 1.6 fusion.79
  85.3 1.7 fusion.80
  87.4 1.6 fusion.79
  89.0 2.9 fusion.80
  92.4 1.6 fusion.79
  94.0 2.9 fusion.80
  97.3 1.6 fusion.79
  98.9 2.9 fusion.80
  102.3 1.6 fusion.79
  103.9 2.9 fusion.80
  107.2 1.6 fusion.79
  108.8 2.9 fusion.80
  112.2 1.6 fusion.79
  113.8 2.9 fusion.80
  117.1 1.6 fusion.79
  118.7 2.9 fusion.80
  121.7 2.5 copy.49
  124.3 6.4 copy.46
  132.3 36.8 %reduce-scatter.5.cloned.1.call-done = f32[128,256]{1,0:T(8,128)} async-done(((f32[1024,256]{1,0:T(8,128)}), f32[128,256]{1,0:T(8,128)}) %reduce-scatter.5.cloned.1.call-update) | async-done | bytes 131088 | tf_op jit(solution)/shard_map/reduce_scatter | solution.py:78
  169.1 1.9 fusion.31
  171.1 20.9 %all_gather.7 = bf16[1024,256]{1,0:T(8,128)(2,1)S(1)} all-gather(bf16[128,256]{1,0:T(8,128)(2,1)S(1)} %convolution_convert_fusion.2), channel_id=1, replica_groups=mesh['loop'=96,'rep'=8] {'rep'}, dimensions={0}, use_global_device_ids=true | all-gather | bytes 589824 | tf_op jit(solution)/shard_map/all_gather | solution.py:89
  192.1 1.1 copy.50
  193.2 53.3 %while.29 = (s32[]{:T(128)}, f32[24,128,256]{2,0,1:T(8,128)S(1)}, bf16[128,24]{1,0:T(8,128)(2,1)}, bf16[128,128,128]{1,2,0:T(8,128)(2,1)}, bf16[128,8]{0,1:T(8,1...) while((s32[]{:T(128)}, f32[24,128,256]{2,0,1:T(8,128)S(1)}, ...), condition=%wide.region_5.0_spmd.clone, body=%wide.region_4.0_spmd.clone.sunk | while | flops 169869312 | bytes 11540657 | solution.py:114
  193.2 1.6 convolution_convert_fusion.6
  194.8 2.6 fusion.87
  197.3 2.5 select_add_fusion.2
  199.8 1.6 convolution_convert_fusion.6
  201.4 2.6 fusion.87
  204.0 2.5 select_add_fusion.2
  206.5 1.6 convolution_convert_fusion.6
  208.1 2.6 fusion.87
  210.7 2.5 select_add_fusion.2
  213.2 1.6 convolution_convert_fusion.6
  214.8 2.6 fusion.87
  217.3 2.5 select_add_fusion.2
  219.8 1.6 convolution_convert_fusion.6
  221.4 2.6 fusion.87
  224.0 2.5 select_add_fusion.2
  226.5 1.6 convolution_convert_fusion.6
  228.1 2.6 fusion.87
  230.7 2.5 select_add_fusion.2
  233.2 1.6 convolution_convert_fusion.6
  234.8 2.6 fusion.87
  237.3 2.5 select_add_fusion.2
  239.9 1.6 convolution_convert_fusion.6
  241.4 2.6 fusion.87
  244.0 2.5 select_add_fusion.2
  246.7 1.5 copy.51
  249.6 1.2 dynamic-slice
  250.8 96.9 %all-reduce.6.cloned.1.call-done = bf16[3,8,128,256]{3,2,1,0:T(8,128)(2,1)} async-done(((bf16[3,8,128,256]{3,2,1,0:T(8,128)(2,1)}), bf16[3,8,128,256]{3,2,1,0:T(8,128)(2,1)}) %all-reduce.6.cloned.1.call-update) | async-done | bytes 1572880
  347.7 1.4 dynamic-slice_bitcast_fusion.1
  349.1 4.7 collective-permute-start.3
  353.9 1.3 collective-permute-start.2
  355.2 460.1 %all-reduce.4.cloned.1.call-done = f32[2,256,256]{1,2,0:T(8,128)} async-done(((f32[2,256,256]{1,2,0:T(8,128)}), f32[2,256,256]{1,2,0:T(8,128)}) %all-reduce.4.cloned.1.call-update) | async-done | bytes 524304 | tf_op jit(solution)/shard_map/psum | solution.py:97
  815.2 1.1 broadcast_multiply_fusion
  817.3 2.2 add_convert_fusion
  (44 shorter events, 10.1 us)
Async XLA Ops:
  7.2 161.9 %copy-start = (bf16[256,256]{1,0:T(8,128)(2,1)S(1)}, bf16[256,256]{1,0:T(8,128)(2,1)}, u32[]{:S(2)}) copy-start(bf16[256,256]{1,0:T(8,128)(2,1)} %param.16) | copy-start | bytes 393220
  7.2 73.8 %all-gather.3.cloned.1.call-start = ((), (), s32[]{:S(2)}) async-start(), calls=%async_computation.3 | async-start | bytes 1769472 | tf_op jit(solution)/shard_map/all_gather | solution.py:44
  7.2 6.8 collective-permute-start.1
  8.5 7.1 collective-permute-start
  17.2 151.9 %reduce-scatter.5.cloned.1.call-start = ((), (), s32[]{:S(2)}) async-start(), calls=%async_computation.1 | async-start | bytes 1179648 | tf_op jit(solution)/shard_map/reduce_scatter | solution.py:78
  124.2 223.5 %all-reduce.6.cloned.1.call-start = ((), (), s32[]{:S(2)}) async-start(), calls=%async_computation.4 | async-start | bytes 3145728
  124.3 7.2 copy-start.1
  124.3 7.2 copy-start.2
  246.7 1.8 copy-start.3
  248.2 567.0 %all-reduce.4.cloned.1.call-start = ((), (), s32[]{:S(2)}) async-start(), calls=%async_computation.2 | async-start | bytes 1048576 | tf_op jit(solution)/shard_map/psum | solution.py:97
  349.1 468.2 %collective-permute-start.3 = (bf16[128,256]{1,0:T(8,128)(2,1)S(1)}, bf16[128,256]{1,0:T(8,128)(2,1)S(1)}, u32[]{:S(2)}, u32[]{:S(2)}) collective-permute-start(bf16[128,256]{1,0:T(8,128)(2,1)S(1)} %get-tuple-element.353), channel_id=1, source_target_pairs={{0,8},{8,16},{16,24},{24,32},{32,40},{40,48},{48,56},{56,64},{64,7... | collective-permute-start | bytes 196616 | tf_op jit(solution)/shard_map/ppermute | solution.py:14
  353.9 463.5 %collective-permute-start.2 = (bf16[128,256]{1,0:T(8,128)(2,1)S(1)}, bf16[128,256]{1,0:T(8,128)(2,1)S(1)}, u32[]{:S(2)}, u32[]{:S(2)}) collective-permute-start(bf16[128,256]{1,0:T(8,128)(2,1)S(1)} %get-tuple-element.352), channel_id=1, source_target_pairs={{8,0},{16,8},{24,16},{32,24},{40,32},{48,40},{56,48},{64,56},{72,6... | collective-permute-start | bytes 196616 | tf_op jit(solution)/shard_map/ppermute | solution.py:14
Sparse Core Ops, SparseCore 0:
  17.3 63.6 all-gather.2
  124.3 44.6 reduce-scatter.4
  248.3 99.3 all-reduce.5
  353.5 461.6 all-reduce.3
where the time goes:
time: 828 us; the launch traced here: 826 us
  waiting for transfers between devices  656 us (79%)
  matrix products  96.9 us (12%)
  blocking collectives  20.9 us (3%)
  local copies, waits for them, and re-layouts  19.5 us (2%)
  between operations  13.9 us (2%)
  starting transfers between devices  12.9 us (2%)
    psum x1, waiting for transfers between devices, on_device(): weight_grads = lax.psum(grad_terms, ('loop', 'rep')) * norm_scale  460 us
    unnamed x5, waiting for transfers between devices  96.9 us
    all_gather x1, waiting for transfers between devices, on_device(): lax.all_gather(band_stack, 'rep', axis=1, tiled=True)  60.3 us
    reduce_scatter x1, waiting for transfers between devices, on_device(): lax.psum_scatter(partial_rows, 'rep', scatter_dimension=0, tiled=True)  36.8 us
    dot_general x8, matrix products, forward_turn(): return running + jnp.einsum('sr,saf->raf', weights, products)  22.1 us
    all_gather x1, blocking collectives, on_device(): kernel_grad = lax.all_gather(own_grad, 'rep', axis=0, tiled=True)  20.9 us
    dot_general x8, matrix products, backward_turn(): jnp.einsum('sab,saf->sbf', tile_block, left_rows, preferred_element_type=...  20.5 us
    dot_general x8, matrix products, backward_turn(): return running + jnp.einsum('so,sbf->obf', targets, products)  19.9 us
  transfers between devices with their start and end apart: 8, of which 5 were waited for; matrix products, arithmetic and copies ran while one was open for 2% of the time, Pallas kernels for 0%

commit v1 on v0

v1 whole, which is shorter than its diff:
```python
import math

import jax
import jax.numpy as jnp
from jax import lax
from jax.experimental import pallas as pl
from jax.experimental.pallas import tpu as pltpu
from jax.sharding import PartitionSpec as P

MESH = pl.DeviceIdType.MESH
BF16 = jnp.bfloat16
F32 = jnp.float32

NL, NX, NY, NH = 3, 4, 8, 4
BANDS = NL * NX * NY
REPS = NH * 2
TILE = 128
FEAT = 256
SLOTS = 128
SPAN = 3
ROWS = REPS * TILE


class Sems:
    def __init__(self):
        self.count = 0

    def take(self, number=1):
        first = self.count
        self.count += number
        return first


def sem_plan():
    sems = Sems()
    plan = {}
    for name, number in (
        ("a_h", 4), ("a_sib", 4), ("a_next", 4), ("a_prev", 4), ("a_sib_prev", 4), ("a_sib_next", 4),
        ("c_sib", 4), ("c_h", 4), ("e_h", 4), ("e_sib", 4),
        ("g_sib", 6), ("g_l", 4), ("g_h", 4),
        ("w_sib", 1), ("w_h", 4), ("w_y", 8), ("w_x", 4), ("w_l", 3),
        ("v_y", 8), ("v_h", 4), ("v_sib", 4),
    ):
        plan[name] = sems.take(number)
    return plan, sems.count


PLAN, N_SEMS = sem_plan()


def dot(a, b):
    return jnp.dot(a, b, preferred_element_type=F32)


def dot_nt(a, b):
    return lax.dot_general(a, b, (((1,), (1,)), ((), ())), preferred_element_type=F32)


def dot_tn(a, b):
    return lax.dot_general(a, b, (((0,), (0,)), ((), ())), preferred_element_type=F32)


def kernel(
    slot_ref, feat_ref, ws_ref, wk_ref, cot_ref, tiles_hbm,
    out_ref, fg_ref, wg_ref,
    tiles, a_mat, f_buf, p_acc, c_send, c_sib, c_chip, c_recv,
    g_t, r_own, r_send, r_sib, r_chip, r_l, r_hs, r_h,
    w_f32, w_send, w_sib, w2_send, w2_recv, w3_src, w3_recv, w4_all, w5_all, w6_all, w7_all,
    tile_sem, ssem, rsem,
):
    loop = lax.axis_index("loop")
    rep = lax.axis_index("rep")
    core = lax.rem(rep, 2)
    other = 1 - core
    h = lax.div(rep, 2)
    l = lax.rem(loop, NL)
    x = lax.rem(lax.div(loop, NL), NX)
    y = lax.div(loop, NL * NX)

    def turn(value, step, count):
        return lax.rem(value + (step % count), count)

    h_next = lax.rem(h + jnp.where(l == NL - 1, 1, 0), NH)
    h_prev = lax.rem(h + jnp.where(l == 0, NH - 1, 0), NH)
    sib_dev = (loop, h * 2 + other)
    next_dev = (lax.rem(loop + 1, BANDS), h_next * 2 + core)
    prev_dev = (lax.rem(loop + BANDS - 1, BANDS), h_prev * 2 + core)
    h_dev = {k: (loop, turn(h, k, NH) * 2 + core) for k in range(1, NH)}
    y_dev = {k: ((turn(y, k, NY) * NX + x) * NL + l, rep) for k in range(1, NY)}
    x_dev = {k: ((y * NX + turn(x, k, NX)) * NL + l, rep) for k in range(1, NX)}
    l_dev = {k: ((y * NX + x) * NL + turn(l, k, NL), rep) for k in range(1, NL)}

    started = []

    def copy(src, dst, name, index, device):
        at = PLAN[name] + index
        return pltpu.make_async_remote_copy(
            src_ref=src, dst_ref=dst, send_sem=ssem.at[at], recv_sem=rsem.at[at],
            device_id=device, device_id_type=MESH,
        )

    def send(src, dst, name, index, device):
        one = copy(src, dst, name, index, device)
        one.start()
        started.append(one)

    def arrived(landing, name, index, device):
        copy(landing, landing, name, index, device).wait_recv()

    tiles_in = [
        pltpu.make_async_copy(tiles_hbm.at[0, pl.ds(q * 32, 32)], tiles.at[pl.ds(q * 32, 32)], tile_sem.at[q])
        for q in range(4)
    ]
    for one in tiles_in:
        one.start()

    barrier = pltpu.get_barrier_semaphore()
    partners = [sib_dev, next_dev, prev_dev]
    for group in (h_dev, y_dev, x_dev, l_dev):
        partners.extend(group.values())
    for device in partners:
        pl.semaphore_signal(barrier, inc=1, device_id=device, device_id_type=MESH)
    pl.semaphore_wait(barrier, len(partners))

    mine = f_buf.at[1, core, h]
    for k in (2, 1, 3):
        send(feat_ref, mine, "a_h", k, h_dev[k])
    send(feat_ref, f_buf.at[0, core, h], "a_next", 0, next_dev)
    send(feat_ref, f_buf.at[2, core, h], "a_prev", 0, prev_dev)
    send(feat_ref, mine, "a_sib", 0, sib_dev)
    f_buf[1, core, h] = feat_ref[...]

    tiles[SLOTS] = jnp.zeros((TILE, TILE), BF16)
    for one in tiles_in:
        one.wait()

    def assemble(b, carry):
        row = pl.multiple_of(b * TILE, TILE)
        for c in range(SPAN * REPS):
            at = slot_ref[b, c]
            a_mat[c // 2, pl.ds(row, TILE), (c % 2) * TILE:(c % 2 + 1) * TILE] = tiles[at]
        return carry

    lax.fori_loop(0, REPS, assemble, 0)

    for k in (1, 3, 2):
        behind = turn(h, -k, NH)
        here = f_buf.at[1, core, behind]
        arrived(here, "a_h", k, h_dev[k])
        send(here, f_buf.at[0, core, behind], "a_next", k, next_dev)
        send(here, f_buf.at[2, core, behind], "a_prev", k, prev_dev)
        send(here, here, "a_sib", k, sib_dev)
    for k in range(NH):
        arrived(f_buf.at[1, other, turn(h, -k, NH)], "a_sib", k, sib_dev)

    def forward_part(j, m):
        rows = pl.ds(pl.multiple_of(m * 256, 256), 256)
        left = jnp.concatenate([a_mat[4 * j + n, rows, :] for n in range(4)], axis=1)
        return dot(left, f_buf[j].reshape(ROWS, FEAT))

    def forward_own(m, carry):
        p_acc[pl.ds(2 * m, 2)] = forward_part(1, m).reshape(2, TILE, FEAT)
        return carry

    lax.fori_loop(0, 4, forward_own, 0)
    self_part = dot(feat_ref[...], ws_ref[...])

    for k in (0, 1, 3, 2):
        before = f_buf.at[0, core, turn(h_prev, -k, NH)]
        arrived(before, "a_next", k, prev_dev)
        send(before, before, "a_sib_prev", k, sib_dev)
        after = f_buf.at[2, core, turn(h_next, -k, NH)]
        arrived(after, "a_prev", k, next_dev)
        send(after, after, "a_sib_next", k, sib_dev)
    for k in range(NH):
        arrived(f_buf.at[0, other, turn(h_prev, -k, NH)], "a_sib_prev", k, sib_dev)
        arrived(f_buf.at[2, other, turn(h_next, -k, NH)], "a_sib_next", k, sib_dev)

    def forward_rest(m):
        both = pl.ds(2 * m, 2)
        return p_acc[both] + (forward_part(0, m) + forward_part(2, m)).reshape(2, TILE, FEAT)

    def forward_sibling(t, carry):
        c_send[pl.ds(2 * t, 2)] = forward_rest(other * 2 + t).astype(BF16)
        return carry

    lax.fori_loop(0, 2, forward_sibling, 0)
    for k in (2, 1, 3, 0):
        send(c_send.at[turn(h, k, NH)], c_sib.at[k], "c_sib", k, sib_dev)

    def forward_mine(t, carry):
        m = core * 2 + t
        p_acc[pl.ds(2 * m, 2)] = forward_rest(m)
        return carry

    lax.fori_loop(0, 2, forward_mine, 0)
    for k in (2, 1, 3):
        arrived(c_sib.at[k], "c_sib", k, sib_dev)
        c_chip[k] = (p_acc[core * NH + turn(h, k, NH)] + c_sib[k].astype(F32)).astype(BF16)
        send(c_chip.at[k], c_recv.at[k], "c_h", k, h_dev[k])
    arrived(c_sib.at[0], "c_sib", 0, sib_dev)
    kernel_sum = p_acc[core * NH + h] + c_sib[0].astype(F32)
    for k in (1, 3, 2):
        arrived(c_recv.at[k], "c_h", k, h_dev[k])
        kernel_sum = kernel_sum + c_recv[k].astype(F32)
    kernel_rows = kernel_sum.astype(BF16)

    preact = self_part + dot(kernel_rows, wk_ref[...])
    root = math.sqrt(2.0 / math.pi)
    square = preact * preact
    bend = jnp.tanh(root * (preact + 0.044715 * (square * preact)))
    half = 0.5 * (1.0 + bend)
    out_ref[...] = (preact * half).astype(BF16)
    slope = half + 0.5 * preact * (1.0 - bend * bend) * (root * (1.0 + 3.0 * 0.044715 * square))
    grad_pre = (cot_ref[...].astype(F32) * slope).astype(BF16)

    g_t[core, h] = dot_nt(wk_ref[...], grad_pre).astype(BF16)
    mine = g_t.at[core, h]
    for k in (2, 1, 3):
        send(mine, mine, "e_h", k, h_dev[k])
    send(mine, mine, "e_sib", 0, sib_dev)

    w_f32[0] = dot_tn(feat_ref[...], grad_pre)
    w_f32[1] = dot_tn(kernel_rows, grad_pre)
    w_send[...] = w_f32[other].astype(BF16)
    send(w_send, w_sib, "w_sib", 0, sib_dev)
    returned = dot_nt(ws_ref[...], grad_pre)

    for k in (1, 3, 2):
        here = g_t.at[core, turn(h, -k, NH)]
        arrived(here, "e_h", k, h_dev[k])
        send(here, here, "e_sib", k, sib_dev)

    arrived(w_sib, "w_sib", 0, sib_dev)

    def chip_rows(block):
        rows = pl.ds(pl.multiple_of(block * 64, 64), 64)
        return w_f32[core, rows, :] + w_sib[rows, :].astype(F32)

    for k in range(1, NH):
        w2_send[k] = chip_rows(turn(h, k, NH)).astype(BF16)
        send(w2_send.at[k], w2_recv.at[k], "w_h", k, h_dev[k])

    for k in range(NH):
        arrived(g_t.at[other, turn(h, -k, NH)], "e_sib", k, sib_dev)

    def backward_part(j, n):
        left = jnp.concatenate([g_t[c, b] for c in range(2) for b in range(NH)], axis=1)
        return dot(left, a_mat[4 * j + n])

    def backward_band(j):
        def for_sibling(t, carry):
            part = backward_part(j, other * 2 + t).astype(BF16)
            r_send[j, 2 * t] = part[:, :TILE]
            r_send[j, 2 * t + 1] = part[:, TILE:]
            return carry

        lax.fori_loop(0, 2, for_sibling, 0)
        for t in range(2):
            two = pl.ds(2 * t, 2)
            send(r_send.at[j, two], r_sib.at[j, two], "g_sib", 2 * j + t, sib_dev)

        def for_me(t, carry):
            part = backward_part(j, core * 2 + t)
            r_own[j, 2 * t] = part[:, :TILE]
            r_own[j, 2 * t + 1] = part[:, TILE:]
            return carry

        lax.fori_loop(0, 2, for_me, 0)

    def to_beside(j, device):
        for t in range(2):
            two = pl.ds(2 * t, 2)
            arrived(r_sib.at[j, two], "g_sib", 2 * j + t, sib_dev)
            r_chip[j // 2, two] = (r_own[j, two] + r_sib[j, two].astype(F32)).astype(BF16)
            send(r_chip.at[j // 2, two], r_l.at[j // 2, two], "g_l", j + t, device)

    backward_band(0)
    backward_band(2)
    to_beside(0, prev_dev)
    to_beside(2, next_dev)

    for k in range(1, NH):
        arrived(w2_recv.at[k], "w_h", k, h_dev[k])
    part = chip_rows(h)
    for k in range(1, NH):
        part = part + w2_recv[k].astype(F32)
    for q in range(NY):
        w3_src[q] = part[(q // 2) * 16:(q // 2 + 1) * 16, (q % 2) * 128:(q % 2 + 1) * 128]
    for k in range(1, NY):
        send(w3_src.at[turn(y, k, NY)], w3_recv.at[k], "w_y", k, y_dev[k])

    backward_band(1)

    for k in range(1, NY):
        arrived(w3_recv.at[k], "w_y", k, y_dev[k])
    part = w3_src[y]
    for k in range(1, NY):
        part = part + w3_recv[k]
    w4_all[x] = part
    for k in range(1, NX):
        send(w4_all.at[x], w4_all.at[x], "w_x", k, x_dev[k])

    for t in range(2):
        arrived(r_sib.at[1, pl.ds(2 * t, 2)], "g_sib", 2 + t, sib_dev)
    r_own[1] = r_own[1] + r_sib[1].astype(F32)

    for k in range(1, NX):
        arrived(w4_all.at[turn(x, -k, NX)], "w_x", k, x_dev[k])
    part = w4_all[0]
    for q in range(1, NX):
        part = part + w4_all[q]
    w5_all[l] = part
    for k in range(1, NL):
        send(w5_all.at[l], w5_all.at[l], "w_l", k, l_dev[k])

    for t in range(2):
        two = pl.ds(2 * t, 2)
        arrived(r_l.at[0, two], "g_l", t, next_dev)
        arrived(r_l.at[1, two], "g_l", 2 + t, prev_dev)

    def summed(block):
        return r_own[1, block] + (r_l[0, block].astype(F32) + r_l[1, block].astype(F32))

    for k in (2, 1, 3):
        r_hs[k] = summed(turn(h, k, NH)).astype(BF16)
        send(r_hs.at[k], r_h.at[k], "g_h", k, h_dev[k])
    returned = returned + summed(h)

    for k in range(1, NL):
        arrived(w5_all.at[turn(l, -k, NL)], "w_l", k, l_dev[k])
    w6_all[y] = w5_all[0] + w5_all[1] + w5_all[2]
    for k in range(1, NY):
        send(w6_all.at[y], w6_all.at[y], "v_y", k, y_dev[k])
    for k in range(1, NY):
        arrived(w6_all.at[turn(y, -k, NY)], "v_y", k, y_dev[k])
    w7_all[core, h] = jnp.concatenate(
        [jnp.concatenate([w6_all[2 * q], w6_all[2 * q + 1]], axis=1) for q in range(NY // 2)], axis=0
    ).astype(BF16)
    mine = w7_all.at[core, h]
    for k in (2, 1, 3):
        send(mine, mine, "v_h", k, h_dev[k])
    send(mine, mine, "v_sib", 0, sib_dev)

    for k in (1, 3, 2):
        arrived(r_h.at[k], "g_h", k, h_dev[k])
        returned = returned + r_h[k].astype(F32)
    fg_ref[...] = returned.T.astype(BF16)

    for k in (1, 3, 2):
        here = w7_all.at[core, turn(h, -k, NH)]
        arrived(here, "v_h", k, h_dev[k])
        send(here, here, "v_sib", k, sib_dev)
    scale = 1.0 / math.sqrt(TILE * REPS * BANDS)
    for k in range(NH):
        arrived(w7_all.at[other, turn(h, -k, NH)], "v_sib", k, sib_dev)
    wg_ref[...] = w7_all[...].astype(F32).reshape(2, FEAT, FEAT) * scale

    for one in started:
        one.wait_send()


def scratch():
    return [
        pltpu.VMEM((SLOTS + 1, TILE, TILE), BF16),
        pltpu.VMEM((SPAN * REPS // 2, ROWS, 2 * TILE), BF16),
        pltpu.VMEM((SPAN, 2, NH, TILE, FEAT), BF16),
        pltpu.VMEM((REPS, TILE, FEAT), F32),
        pltpu.VMEM((NH, TILE, FEAT), BF16),
        pltpu.VMEM((NH, TILE, FEAT), BF16),
        pltpu.VMEM((NH, TILE, FEAT), BF16),
        pltpu.VMEM((NH, TILE, FEAT), BF16),
        pltpu.VMEM((2, NH, FEAT, TILE), BF16),
        pltpu.VMEM((SPAN, NH, FEAT, TILE), F32),
        pltpu.VMEM((SPAN, NH, FEAT, TILE), BF16),
        pltpu.VMEM((SPAN, NH, FEAT, TILE), BF16),
        pltpu.VMEM((2, NH, FEAT, TILE), BF16),
        pltpu.VMEM((2, NH, FEAT, TILE), BF16),
        pltpu.VMEM((NH, FEAT, TILE), BF16),
        pltpu.VMEM((NH, FEAT, TILE), BF16),
        pltpu.VMEM((2, FEAT, FEAT), F32),
        pltpu.VMEM((FEAT, FEAT), BF16),
        pltpu.VMEM((FEAT, FEAT), BF16),
        pltpu.VMEM((NH, 64, FEAT), BF16),
        pltpu.VMEM((NH, 64, FEAT), BF16),
        pltpu.VMEM((NY, 16, 128), F32),
        pltpu.VMEM((NY, 16, 128), F32),
        pltpu.VMEM((NX, 16, 128), F32),
        pltpu.VMEM((NL, 16, 128), F32),
        pltpu.VMEM((NY, 16, 128), F32),
        pltpu.VMEM((2, NH, 64, FEAT), BF16),
        pltpu.SemaphoreType.DMA((4,)),
        pltpu.SemaphoreType.DMA((N_SEMS,)),
        pltpu.SemaphoreType.DMA((N_SEMS,)),
    ]


def slot_table(row_starts, column_block):
    band = lax.axis_index("loop")
    slots = jnp.arange(SLOTS, dtype=jnp.int32)
    row = jnp.sum((row_starts[0, 1:REPS, None] <= slots[None, :]).astype(jnp.int32), axis=0)
    column = column_block[0] - (band - 1) * REPS
    side, within = column // REPS, column % REPS
    key = ((row % 2) * NH + row // 2) * (SPAN * REPS) + side * REPS + (within % 2) * NH + within // 2
    key = jnp.where(slots < row_starts[0, REPS], key, -1)
    places = jnp.arange(REPS * SPAN * REPS, dtype=jnp.int32)
    found = jnp.where(key[None, :] == places[:, None], slots[None, :] - SLOTS, 0)
    return (jnp.sum(found, axis=1) + SLOTS).reshape(REPS, SPAN * REPS)


def on_device(features, kernel_tiles, row_starts, column_block, self_weight, kernel_weight, cotangent):
    vmem = pl.BlockSpec(memory_space=pltpu.VMEM)
    return pl.pallas_call(
        kernel,
        out_shape=(
            jax.ShapeDtypeStruct((TILE, FEAT), BF16),
            jax.ShapeDtypeStruct((TILE, FEAT), BF16),
            jax.ShapeDtypeStruct((2, FEAT, FEAT), F32),
        ),
        in_specs=[pl.BlockSpec(memory_space=pltpu.SMEM), vmem, vmem, vmem, vmem, pl.BlockSpec(memory_space=pl.ANY)],
        out_specs=(vmem, vmem, vmem),
        scratch_shapes=scratch(),
        compiler_params=pltpu.CompilerParams(
            collective_id=0, has_side_effects=True, vmem_limit_bytes=48 * 1024 * 1024
        ),
    )(slot_table(row_starts, column_block), features, self_weight, kernel_weight, cotangent, kernel_tiles)


def solution(mesh):
    split = P(("loop", "rep"), None)
    return jax.shard_map(
        on_device,
        mesh=mesh,
        in_specs=(split, P(("loop", "rep"), None, None, None), split, split, P(), P(), split),
        out_specs=(split, split, P()),
        check_vma=False,
    )
```

time: 828 us -> 114 us (0.14)
  waiting for transfers between devices: 656 us -> 0 us
  Pallas kernels: 0 us -> 102 us
  matrix products: 96.9 us -> 0 us
  blocking collectives: 20.9 us -> 0 us
  between operations: 13.9 us -> 0.67 us
  starting transfers between devices: 12.9 us -> 0 us
  local copies, waits for them, and re-layouts: 19.5 us -> 9.78 us
    psum x1 -> x0, waiting for transfers between devices: 460 us -> none  [on_device(): weight_grads = lax.psum(grad_terms, ('loop', 'rep')) * norm_scale]
    pallas_call x0 -> x1, Pallas kernels: none -> 102 us  [on_device(): pl.pallas_call(kernel, out_shape=(jax.ShapeDtypeStruct((TILE, FEAT), BF16...]
    unnamed x5 -> x0, waiting for transfers between devices: 96.9 us -> none
    dot_general x54 -> x0, matrix products: 96.9 us -> none  [the longest x8 22.1 us: forward_turn(): return running + jnp.einsum('sr,saf->raf', weights, products)]
    all_gather x1 -> x0, waiting for transfers between devices: 60.3 us -> none  [on_device(): lax.all_gather(band_stack, 'rep', axis=1, tiled=True)]
    reduce_scatter x1 -> x0, waiting for transfers between devices: 36.8 us -> none  [on_device(): lax.psum_scatter(partial_rows, 'rep', scatter_dimension=0, tiled=True)]
    all_gather x1 -> x0, blocking collectives: 20.9 us -> none  [on_device(): kernel_grad = lax.all_gather(own_grad, 'rep', axis=0, tiled=True)]
    ppermute x4 -> x0, starting transfers between devices: 12.8 us -> none  [from_behind(): lax.ppermute(value, axis, [(source, source + steps) for source in range(l...]
  transfers between devices with their start and end apart: 8 -> 0, of which waited for: 5 -> 0; matrix products, arithmetic and copies ran while one was open for 2% -> 0% of each run, Pallas kernels for 0% -> 0%
where the time goes in v1:
time: 114 us
  Pallas kernels  102 us (89%)
  local copies, waits for them, and re-layouts  9.78 us (9%)
  other arithmetic  1.53 us (1%)
    pallas_call x1, Pallas kernels, on_device(): pl.pallas_call(kernel, out_shape=(jax.ShapeDtypeStruct((TILE, FEAT), BF16...  102 us
    unnamed x13, local copies, waits for them, and re-layouts  7.74 us

profile of v1, /device:TPU:1, one launch (start us, length us, event | category | flops | bytes accessed | tf_op | source)
XLA Modules:
  0.0 113.5 jit_solution(8449524026129029677)
XLA Ops:
  0.6 1.2 %slice.6 = s32[1,1]{1,0:T(1,128)} slice(s32[1,9]{1,0:T(1,128)} %param.9), slice={[0:1], [8:9]} | slice | bytes 8 | tf_op jit(solution)/shard_map/slice | solution.py:405
  1.9 0.7 slice_bitcast_fusion
  2.6 0.1 convert_reduce_fusion
  2.7 1.3 %fusion = s32[128]{0:T(128)S(1)} fusion(s32[1,128]{1,0:T(1,128)} %param.10, s32[128]{0:T(128)S(1)} %convert_reduce_fusion, s32[]{:T(128)S(6)} %mul.38, s32[]{:T(128)} %bitcast), kind=kLoop, calls=%fused_computation.20 | loop fusion | flops 8704 | bytes 1544 | tf_op jit(solution)/shard_map/eq | solution.py:407
  4.0 0.1 select_reduce_fusion
  4.1 0.1 add.83.slot_ref
  4.2 0.0 copy-start
  4.2 2.2 %copy-done = bf16[1,128,128,128]{3,2,1,0:T(8,128)(2,1)S(1)} copy-done((bf16[1,128,128,128]{3,2,1,0:T(8,128)(2,1)S(1)}, bf16[1,128,128,128]{3,2,1,0:T(8,128)(2,1)}, u32[]{:S(2)}) %copy-start) | copy-done | bytes 4194328
  6.4 0.0 copy-start.1
  6.4 0.9 copy-done.1
  7.3 0.0 copy-start.2
  7.3 0.9 copy-done.2
  8.2 0.0 copy-start.3
  8.2 0.8 copy-done.3
  9.1 0.0 copy-start.4
  9.1 0.8 copy-done.4
  9.9 101.5 %shard_map.94 = (bf16[128,256]{1,0:T(8,128)(2,1)S(1)}, bf16[128,256]{1,0:T(8,128)(2,1)S(1)}, f32[2,256,256]{2,1,0:T(8,128)S(1)}) custom-call(s32[8,24]{1,0:T(8,128)S(1)} %add.83.slot_ref, bf16[128,256]{1,0:T(8,128)(2,1)S(1)} %copy-done.3, bf16[256,256]{1,0:T(8,128)(2,1)S(1)} %copy-done.1, bf16[256,256]{1,0:T(8,128)(2,1)S(1)} %copy-done.2, ...), custom_call_target="tpu_custom_call" | custom-call | tf_op jit(solution)/shard_map/pallas_call | solution.py:413
  111.5 0.6 copy.13
  112.1 0.6 copy.14
  112.7 0.8 copy.15
  (2 shorter events, 0.0 us)
Async XLA Ops:
  4.2 2.2 %copy-start = (bf16[1,128,128,128]{3,2,1,0:T(8,128)(2,1)S(1)}, bf16[1,128,128,128]{3,2,1,0:T(8,128)(2,1)}, u32[]{:S(2)}) copy-start(bf16[1,128,128,128]{3,2,1,0:T(8,128)(2,1)} %tiles_hbm.1) | copy-start | bytes 12582916
  6.4 0.9 copy-start.1
  7.3 0.9 copy-start.2
  8.2 0.8 copy-start.3
  9.1 0.8 copy-start.4

commit v2 on v1

v2 whole, which is shorter than its diff:
```python
import math

import jax
import jax.numpy as jnp
from jax import lax
from jax.experimental import pallas as pl
from jax.experimental.pallas import tpu as pltpu
from jax.sharding import PartitionSpec as P

MESH = pl.DeviceIdType.MESH
BF16 = jnp.bfloat16
F32 = jnp.float32

NL, NX, NY, NH = 3, 4, 8, 4
BANDS = NL * NX * NY
REPS = NH * 2
TILE = 128
FEAT = 256
SLOTS = 128
SPAN = 3
ROWS = REPS * TILE


def sem_plan():
    plan, count = {}, 0
    for name, number in (
        ("a_h", 4), ("a_sib", 4), ("a_next", 4), ("a_prev", 4), ("a_sib_prev", 4), ("a_sib_next", 4),
        ("c_sib", 4), ("c_h", 4), ("e_h", 4), ("e_sib", 4),
        ("g_sib", 12), ("g_l", 8), ("g_h", 4),
        ("w_sib", 1), ("w_y", 8), ("w_x", 4), ("w_h", 4), ("w_l", 3),
        ("v_x", 4), ("v_y", 8), ("v_sib", 1),
    ):
        plan[name] = count
        count += number
    return plan, count


PLAN, N_SEMS = sem_plan()


def dot(a, b):
    return jnp.dot(a, b, preferred_element_type=F32)


def dot_nt(a, b):
    return lax.dot_general(a, b, (((1,), (1,)), ((), ())), preferred_element_type=F32)


def dot_tn(a, b):
    return lax.dot_general(a, b, (((0,), (0,)), ((), ())), preferred_element_type=F32)


def kernel(
    starts_ref, columns_ref, feat_hbm, ws_hbm, wk_hbm, cot_hbm, tiles_hbm,
    out_ref, fg_ref, wg_ref,
    feat_ref, ws_ref, wk_ref, cot_ref, table_v, table,
    tiles, a_mat, f_buf, p_acc, c_send, c_sib, c_chip, c_recv,
    g_t, r_acc, r_own, r_send, r_sib, r_chip, r_l, r_hs, r_h,
    w_f32, w_send, w_sib, wy_send, wy_recv, wx_send, wx_recv, wh_all, wl_all, vx_all, vy_all, v_mat,
    local_sem, ssem, rsem,
):
    loop = lax.axis_index("loop")
    rep = lax.axis_index("rep")
    core = lax.rem(rep, 2)
    other = 1 - core
    h = lax.div(rep, 2)
    l = lax.rem(loop, NL)
    x = lax.rem(lax.div(loop, NL), NX)
    y = lax.div(loop, NL * NX)

    def turn(value, step, count):
        return lax.rem(value + (step % count), count)

    h_next = lax.rem(h + jnp.where(l == NL - 1, 1, 0), NH)
    h_prev = lax.rem(h + jnp.where(l == 0, NH - 1, 0), NH)
    sib_dev = (loop, h * 2 + other)
    next_dev = (lax.rem(loop + 1, BANDS), h_next * 2 + core)
    prev_dev = (lax.rem(loop + BANDS - 1, BANDS), h_prev * 2 + core)
    h_dev = {k: (loop, turn(h, k, NH) * 2 + core) for k in range(1, NH)}
    y_dev = {k: ((turn(y, k, NY) * NX + x) * NL + l, rep) for k in range(1, NY)}
    x_dev = {k: ((y * NX + turn(x, k, NX)) * NL + l, rep) for k in range(1, NX)}
    l_dev = {k: ((y * NX + x) * NL + turn(l, k, NL), rep) for k in range(1, NL)}

    started = []

    def copy(src, dst, name, index, device):
        at = PLAN[name] + index
        return pltpu.make_async_remote_copy(
            src_ref=src, dst_ref=dst, send_sem=ssem.at[at], recv_sem=rsem.at[at],
            device_id=device, device_id_type=MESH,
        )

    def send(src, dst, name, index, device):
        one = copy(src, dst, name, index, device)
        one.start()
        started.append(one)

    def arrived(landing, name, index, device):
        copy(landing, landing, name, index, device).wait_recv()

    feat_in = pltpu.make_async_copy(feat_hbm, feat_ref, local_sem.at[0])
    others_in = [
        pltpu.make_async_copy(src, dst, local_sem.at[1 + at])
        for at, (src, dst) in enumerate(((ws_hbm, ws_ref), (wk_hbm, wk_ref), (cot_hbm, cot_ref)))
    ]
    tiles_in = [
        pltpu.make_async_copy(tiles_hbm.at[0, pl.ds(q * 32, 32)], tiles.at[pl.ds(q * 32, 32)], local_sem.at[4 + q])
        for q in range(4)
    ]
    for one in [feat_in] + tiles_in + others_in:
        one.start()

    barrier = pltpu.get_barrier_semaphore()
    partners = [sib_dev, next_dev, prev_dev]
    for group in (h_dev, y_dev, x_dev, l_dev):
        partners.extend(group.values())
    for device in partners:
        pl.semaphore_signal(barrier, inc=1, device_id=device, device_id_type=MESH)

    slot = lax.broadcasted_iota(jnp.int32, (1, SLOTS), 1)
    row = jnp.zeros((1, SLOTS), jnp.int32)
    for k in range(1, REPS):
        row = row + jnp.where(starts_ref[0, k] <= slot, 1, 0)
    key = row * 32 + (columns_ref[...] - (loop - 1) * REPS)
    key = jnp.where(slot < starts_ref[0, REPS], key, -1)
    key = jnp.broadcast_to(key, (SLOTS, SLOTS)).T
    place = lax.broadcasted_iota(jnp.int32, (SLOTS, SLOTS), 1)
    slot = lax.broadcasted_iota(jnp.int32, (SLOTS, SLOTS), 0) - SLOTS
    for q in range(2):
        found = jnp.sum(jnp.where(key == place + 128 * q, slot, 0), axis=0, keepdims=True)
        table_v[q:q + 1, :] = found + SLOTS
    table_in = pltpu.make_async_copy(table_v, table, local_sem.at[8])
    table_in.start()
    feat_in.wait()
    pl.semaphore_wait(barrier, len(partners))

    mine = f_buf.at[1, h, core]
    for k in (2, 1, 3):
        send(feat_ref, mine, "a_h", k, h_dev[k])
    send(feat_ref, f_buf.at[0, h, core], "a_next", 0, next_dev)
    send(feat_ref, f_buf.at[2, h, core], "a_prev", 0, prev_dev)
    send(feat_ref, mine, "a_sib", 0, sib_dev)
    f_buf[1, h, core] = feat_ref[...]

    tiles[SLOTS] = jnp.zeros((TILE, TILE), BF16)
    table_in.wait()
    for one in tiles_in:
        one.wait()

    def assemble(b, carry):
        rows = pl.ds(pl.multiple_of(b * TILE, TILE), TILE)
        line, first = lax.div(b, 4), lax.rem(b, 4) * 32
        for c in range(SPAN * REPS):
            at = jnp.clip(table[line, first + c], 0, SLOTS)
            a_mat[c // 2, rows, (c % 2) * TILE:(c % 2 + 1) * TILE] = tiles[at]
        return carry

    lax.fori_loop(0, REPS, assemble, 0)
    for one in others_in:
        one.wait()

    def own_block(k):
        return f_buf.at[1, turn(h, -k, NH), core]

    def own_in(k):
        here = own_block(k)
        behind = turn(h, -k, NH)
        arrived(here, "a_h", k, h_dev[k])
        send(here, f_buf.at[0, behind, core], "a_next", k, next_dev)
        send(here, f_buf.at[2, behind, core], "a_prev", k, prev_dev)
        send(here, here, "a_sib", k, sib_dev)

    def beside_in(k):
        before = f_buf.at[0, turn(h_prev, -k, NH), core]
        arrived(before, "a_next", k, prev_dev)
        send(before, before, "a_sib_prev", k, sib_dev)
        after = f_buf.at[2, turn(h_next, -k, NH), core]
        arrived(after, "a_prev", k, next_dev)
        send(after, after, "a_sib_next", k, sib_dev)

    def product(j, at, m):
        rows = pl.ds(pl.multiple_of(m * 256, 256), 256)
        return dot(a_mat[4 * j + at, rows, :], f_buf[j, at].reshape(256, FEAT)).reshape(2, TILE, FEAT)

    def add_own(k, first=False):
        at = turn(h, -k, NH)
        arrived(f_buf.at[1, at, other], "a_sib", k, sib_dev)

        def step(m, carry):
            part = product(1, at, m)
            p_acc[m] = part if first else p_acc[m] + part
            return carry

        lax.fori_loop(0, NH, step, 0)

    def beside_at(k):
        before, after = turn(h_prev, -k, NH), turn(h_next, -k, NH)
        arrived(f_buf.at[0, before, other], "a_sib_prev", k, sib_dev)
        arrived(f_buf.at[2, after, other], "a_sib_next", k, sib_dev)
        return before, after

    def add_beside(k):
        before, after = beside_at(k)

        def step(m, carry):
            p_acc[m] = p_acc[m] + (product(0, before, m) + product(2, after, m))
            return carry

        lax.fori_loop(0, NH, step, 0)

    own_in(1)
    own_in(3)
    beside_in(0)
    add_own(0, first=True)
    own_in(2)
    add_own(1)
    add_own(3)
    beside_in(1)
    beside_in(3)
    add_beside(0)
    add_own(2)
    add_beside(1)
    self_part = dot(feat_ref[...], ws_ref[...])
    beside_in(2)
    add_beside(3)

    before, after = beside_at(2)
    for k in (2, 1, 3, 0):
        m = turn(h, k, NH)
        p_acc[m] = p_acc[m] + (product(0, before, m) + product(2, after, m))
        c_send[k] = p_acc[m, other].astype(BF16)
        send(c_send.at[k], c_sib.at[k], "c_sib", k, sib_dev)
    for k in (2, 1, 3):
        arrived(c_sib.at[k], "c_sib", k, sib_dev)
        c_chip[k] = (p_acc[turn(h, k, NH), core] + c_sib[k].astype(F32)).astype(BF16)
        send(c_chip.at[k], c_recv.at[k], "c_h", k, h_dev[k])
    arrived(c_sib.at[0], "c_sib", 0, sib_dev)
    kernel_sum = p_acc[h, core] + c_sib[0].astype(F32)
    for k in (1, 3, 2):
        arrived(c_recv.at[k], "c_h", k, h_dev[k])
        kernel_sum = kernel_sum + c_recv[k].astype(F32)
    kernel_rows = kernel_sum.astype(BF16)

    preact = self_part + dot(kernel_rows, wk_ref[...])
    root = math.sqrt(2.0 / math.pi)
    square = preact * preact
    bend = jnp.tanh(root * (preact + 0.044715 * (square * preact)))
    half = 0.5 * (1.0 + bend)
    slope = half + 0.5 * preact * (1.0 - bend * bend) * (root * (1.0 + 3.0 * 0.044715 * square))
    grad_pre = (cot_ref[...].astype(F32) * slope).astype(BF16)

    g_t[h, core] = dot_nt(wk_ref[...], grad_pre).astype(BF16)
    mine = g_t.at[h, core]
    for k in (2, 1, 3):
        send(mine, mine, "e_h", k, h_dev[k])
    send(mine, mine, "e_sib", 0, sib_dev)
    out_ref[...] = (preact * half).astype(BF16)

    w_f32[0] = dot_tn(feat_ref[...], grad_pre)
    w_f32[1] = dot_tn(kernel_rows, grad_pre)
    w_send[...] = w_f32[other].astype(BF16)
    send(w_send, w_sib, "w_sib", 0, sib_dev)
    returned = dot_nt(ws_ref[...], grad_pre)

    def gradients(at):
        return jnp.concatenate([g_t[at, 0], g_t[at, 1]], axis=1)

    def back(at, left, n):
        rows = pl.ds(pl.multiple_of(at * 256, 256), 256)
        return dot(left, a_mat[n, rows, :])

    def add_back(k, first=False):
        at = turn(h, -k, NH)
        arrived(g_t.at[at, other], "e_sib", k, sib_dev)
        left = gradients(at)

        def step(n, carry):
            part = back(at, left, n)
            r_acc[n] = part if first else r_acc[n] + part
            return carry

        lax.fori_loop(0, SPAN * NH, step, 0)

    def gradient_in(k):
        here = g_t.at[turn(h, -k, NH), core]
        arrived(here, "e_h", k, h_dev[k])
        send(here, here, "e_sib", k, sib_dev)

    def chip_rows(block):
        rows = pl.ds(pl.multiple_of(block * 32, 32), 32)
        return w_f32[core, rows, :] + w_sib[rows, :].astype(F32)

    arrived(w_sib, "w_sib", 0, sib_dev)
    for k in range(1, NY):
        wy_send[k] = chip_rows(turn(y, k, NY)).astype(BF16)
        send(wy_send.at[k], wy_recv.at[k], "w_y", k, y_dev[k])
    add_back(0, first=True)
    gradient_in(1)
    gradient_in(3)
    add_back(1)
    gradient_in(2)
    for k in range(1, NY):
        arrived(wy_recv.at[k], "w_y", k, y_dev[k])
    part = chip_rows(y)
    for k in range(1, NY):
        part = part + wy_recv[k].astype(F32)
    for q in range(NX):
        wx_send[q] = part[(q // 2) * 16:(q // 2 + 1) * 16, (q % 2) * 128:(q % 2 + 1) * 128]
    for k in range(1, NX):
        send(wx_send.at[turn(x, k, NX)], wx_recv.at[k], "w_x", k, x_dev[k])

    add_back(3)

    for k in range(1, NX):
        arrived(wx_recv.at[k], "w_x", k, x_dev[k])
    part = wx_send[x]
    for k in range(1, NX):
        part = part + wx_recv[k]
    wh_all[h] = part
    for k in (2, 1, 3):
        send(wh_all.at[h], wh_all.at[h], "w_h", k, h_dev[k])

    at = turn(h, -2, NH)
    arrived(g_t.at[at, other], "e_sib", 2, sib_dev)
    left = gradients(at)
    first_core = core == 0

    def backward_band(j):
        for q in range(NH):
            part = r_acc[4 * j + q] + back(at, left, 4 * j + q)
            low, high = part[:, :TILE], part[:, TILE:]
            r_send[j, q] = jnp.where(first_core, high, low).astype(BF16)
            send(r_send.at[j, q], r_sib.at[j, q], "g_sib", 4 * j + q, sib_dev)
            r_own[j, q] = jnp.where(first_core, low, high)

    def to_beside(j, device):
        for q in range(NH):
            arrived(r_sib.at[j, q], "g_sib", 4 * j + q, sib_dev)
            r_chip[j // 2, q] = (r_own[j, q] + r_sib[j, q].astype(F32)).astype(BF16)
            send(r_chip.at[j // 2, q], r_l.at[j // 2, q], "g_l", 2 * j + q, device)

    backward_band(0)
    backward_band(2)
    to_beside(0, prev_dev)
    to_beside(2, next_dev)

    backward_band(1)

    for k in range(1, NH):
        arrived(wh_all.at[turn(h, -k, NH)], "w_h", k, h_dev[k])
    wl_all[l] = (wh_all[0] + wh_all[1]) + (wh_all[2] + wh_all[3])
    for k in range(1, NL):
        send(wl_all.at[l], wl_all.at[l], "w_l", k, l_dev[k])

    for q in range(NH):
        arrived(r_sib.at[1, q], "g_sib", 4 + q, sib_dev)
    r_own[1] = r_own[1] + r_sib[1].astype(F32)

    for k in range(1, NL):
        arrived(wl_all.at[turn(l, -k, NL)], "w_l", k, l_dev[k])
    vx_all[x] = (wl_all[0] + wl_all[1] + wl_all[2]).astype(BF16)
    for k in range(1, NX):
        send(vx_all.at[x], vx_all.at[x], "v_x", k, x_dev[k])
    for q in range(NH):
        arrived(r_l.at[0, q], "g_l", q, next_dev)
        arrived(r_l.at[1, q], "g_l", 4 + q, prev_dev)

    def summed(block):
        return r_own[1, block] + (r_l[0, block].astype(F32) + r_l[1, block].astype(F32))

    for k in (2, 1, 3):
        r_hs[k] = summed(turn(h, k, NH)).astype(BF16)
        send(r_hs.at[k], r_h.at[k], "g_h", k, h_dev[k])
    returned = returned + summed(h)

    for k in range(1, NX):
        arrived(vx_all.at[turn(x, -k, NX)], "v_x", k, x_dev[k])
    vy_all[y] = jnp.concatenate(
        [jnp.concatenate([vx_all[2 * q], vx_all[2 * q + 1]], axis=1) for q in range(NX // 2)], axis=0
    )
    for k in range(1, NY):
        send(vy_all.at[y], vy_all.at[y], "v_y", k, y_dev[k])

    for k in (1, 3, 2):
        arrived(r_h.at[k], "g_h", k, h_dev[k])
        returned = returned + r_h[k].astype(F32)
    fg_ref[...] = returned.T.astype(BF16)

    for k in range(1, NY):
        arrived(vy_all.at[turn(y, -k, NY)], "v_y", k, y_dev[k])
    v_mat[core] = vy_all[...].reshape(FEAT, FEAT)
    send(v_mat.at[core], v_mat.at[core], "v_sib", 0, sib_dev)
    scale = 1.0 / math.sqrt(TILE * REPS * BANDS)
    wg_ref[core] = v_mat[core].astype(F32) * scale
    arrived(v_mat.at[other], "v_sib", 0, sib_dev)
    wg_ref[other] = v_mat[other].astype(F32) * scale

    for one in started:
        one.wait_send()


def scratch():
    return [
        pltpu.VMEM((TILE, FEAT), BF16),
        pltpu.VMEM((FEAT, FEAT), BF16),
        pltpu.VMEM((FEAT, FEAT), BF16),
        pltpu.VMEM((TILE, FEAT), BF16),
        pltpu.VMEM((2, 128), jnp.int32),
        pltpu.SMEM((2, 128), jnp.int32),
        pltpu.VMEM((SLOTS + 1, TILE, TILE), BF16),
        pltpu.VMEM((SPAN * NH, REPS * TILE, 2 * TILE), BF16),
        pltpu.VMEM((SPAN, NH, 2, TILE, FEAT), BF16),
        pltpu.VMEM((NH, 2, TILE, FEAT), F32),
        pltpu.VMEM((NH, TILE, FEAT), BF16),
        pltpu.VMEM((NH, TILE, FEAT), BF16),
        pltpu.VMEM((NH, TILE, FEAT), BF16),
        pltpu.VMEM((NH, TILE, FEAT), BF16),
        pltpu.VMEM((NH, 2, FEAT, TILE), BF16),
        pltpu.VMEM((SPAN * NH, FEAT, 2 * TILE), F32),
        pltpu.VMEM((SPAN, NH, FEAT, TILE), F32),
        pltpu.VMEM((SPAN, NH, FEAT, TILE), BF16),
        pltpu.VMEM((SPAN, NH, FEAT, TILE), BF16),
        pltpu.VMEM((2, NH, FEAT, TILE), BF16),
        pltpu.VMEM((2, NH, FEAT, TILE), BF16),
        pltpu.VMEM((NH, FEAT, TILE), BF16),
        pltpu.VMEM((NH, FEAT, TILE), BF16),
        pltpu.VMEM((2, FEAT, FEAT), F32),
        pltpu.VMEM((FEAT, FEAT), BF16),
        pltpu.VMEM((FEAT, FEAT), BF16),
        pltpu.VMEM((NY, 32, FEAT), BF16),
        pltpu.VMEM((NY, 32, FEAT), BF16),
        pltpu.VMEM((NX, 16, 128), F32),
        pltpu.VMEM((NX, 16, 128), F32),
        pltpu.VMEM((NH, 16, 128), F32),
        pltpu.VMEM((NL, 16, 128), F32),
        pltpu.VMEM((NX, 16, 128), BF16),
        pltpu.VMEM((NY, 32, FEAT), BF16),
        pltpu.VMEM((2, FEAT, FEAT), BF16),
        pltpu.SemaphoreType.DMA((9,)),
        pltpu.SemaphoreType.DMA((N_SEMS,)),
        pltpu.SemaphoreType.DMA((N_SEMS,)),
    ]


def hand_out(*refs):
    results, outputs, held, sem = refs[:3], refs[3:6], refs[6:9], refs[9]
    ins = [pltpu.make_async_copy(results[at], held[at], sem.at[at]) for at in range(3)]
    outs = [pltpu.make_async_copy(held[at], outputs[at], sem.at[3 + at]) for at in range(3)]
    for one in ins:
        one.start()
    for at in range(3):
        ins[at].wait()
        outs[at].start()
    for one in outs:
        one.wait()


def on_device(features, kernel_tiles, row_starts, column_block, self_weight, kernel_weight, cotangent):
    vmem = pl.BlockSpec(memory_space=pltpu.VMEM)
    hbm = pl.BlockSpec(memory_space=pltpu.HBM)
    shapes = (
        jax.ShapeDtypeStruct((TILE, FEAT), BF16),
        jax.ShapeDtypeStruct((TILE, FEAT), BF16),
        jax.ShapeDtypeStruct((2, FEAT, FEAT), F32),
    )
    results = pl.pallas_call(
        kernel,
        out_shape=shapes,
        in_specs=[pl.BlockSpec(memory_space=pltpu.SMEM), vmem, hbm, hbm, hbm, hbm, hbm],
        out_specs=(vmem, vmem, vmem),
        scratch_shapes=scratch(),
        compiler_params=pltpu.CompilerParams(
            collective_id=0, has_side_effects=True, vmem_limit_bytes=64 * 1024 * 1024 - 65536
        ),
    )(row_starts, column_block, features, self_weight, kernel_weight, cotangent, kernel_tiles)
    return pl.pallas_call(
        hand_out,
        out_shape=shapes,
        in_specs=[pl.BlockSpec(memory_space=pl.ANY)] * 3,
        out_specs=(pl.BlockSpec(memory_space=pl.ANY),) * 3,
        scratch_shapes=[pltpu.VMEM(one.shape, one.dtype) for one in shapes] + [pltpu.SemaphoreType.DMA((6,))],
        compiler_params=pltpu.CompilerParams(vmem_limit_bytes=64 * 1024 * 1024 - 65536),
    )(*results)


def solution(mesh):
    split = P(("loop", "rep"), None)
    return jax.shard_map(
        on_device,
        mesh=mesh,
        in_specs=(split, P(("loop", "rep"), None, None, None), split, split, P(), P(), split),
        out_specs=(split, split, P()),
        check_vma=False,
    )
```

time: 114 us -> 98.9 us (0.87)
  local copies, waits for them, and re-layouts: 9.78 us -> 0 us
  Pallas kernels: 102 us -> 97.2 us
  other arithmetic: 1.53 us -> 0 us
    unnamed x13 -> x0, local copies, waits for them, and re-layouts: 7.74 us -> none
    pallas_call x1 -> x2, Pallas kernels: 102 us -> 97.2 us  [the longest x1 95.2 us: on_device(): pl.pallas_call(kernel, out_shape=shapes, in_specs=[pl.BlockSpec(memory_sp...]
    eq x1 -> x0, other arithmetic: 1.32 us -> none  [slot_table(): key[None, :] == places[:, None]]
    slice x1 -> x0, local copies, waits for them, and re-layouts: 1.24 us -> none  [slot_table(): key = jnp.where(slots < row_starts[0, REPS], key, -1)]
where the time goes in v2:
time: 98.9 us; the launch traced here: 97.8 us
  Pallas kernels  97.2 us (98%)
    pallas_call x1, Pallas kernels, on_device(): pl.pallas_call(kernel, out_shape=shapes, in_specs=[pl.BlockSpec(memory_sp...  95.2 us

profile of v2, /device:TPU:1, one launch (start us, length us, event | category | flops | bytes accessed | tf_op | source)
XLA Modules:
  0.0 97.8 jit_solution(1849667275525814524)
XLA Ops:
  0.6 95.2 %shard_map.94 = (bf16[128,256]{1,0:T(8,128)(2,1)}, bf16[128,256]{1,0:T(8,128)(2,1)}, f32[2,256,256]{2,1,0:T(8,128)}) custom-call(s32[1,9]{1,0:T(1,128)} %starts_ref.1, s32[1,128]{1,0:T(1,128)} %columns_ref.1, bf16[128,256]{1,0:T(8,128)(2,1)} %feat_hbm.1, bf16[256,256]{1,0:T(8,128)(2,1)} %ws_hbm.1, bf16[256,256]{1,0:T(8,128)(2,1)} %wk_hbm.1, ...), custom_call_target="tpu_custom_call" | custom-call | tf_op jit(solution)/shard_map/pallas_call | solution.py:466
  95.9 2.0 %shard_map.95 = (bf16[128,256]{1,0:T(8,128)(2,1)}, bf16[128,256]{1,0:T(8,128)(2,1)}, f32[2,256,256]{2,1,0:T(8,128)}) custom-call(bf16[128,256]{1,0:T(8,128)(2,1)} %get-tuple-element.6.refs_0_, bf16[128,256]{1,0:T(8,128)(2,1)} %get-tuple-element.7.refs_1_, f32[2,256,256]{2,1,0:T(8,128)} %get-tuple-element.8.refs_2_), custom_call_target="tpu_custom_call" | custom-call | tf_op jit(solution)/shard_map/pallas_call | solution.py:476

commit v3 on v2

--- a/solution.py
+++ b/solution.py
@@ -28,7 +28,7 @@
         ("c_sib", 4), ("c_h", 4), ("e_h", 4), ("e_sib", 4),
         ("g_sib", 12), ("g_l", 8), ("g_h", 4),
         ("w_sib", 1), ("w_y", 8), ("w_x", 4), ("w_h", 4), ("w_l", 3),
-        ("v_x", 4), ("v_y", 8), ("v_sib", 1),
+        ("v_y", 8), ("v_sib", 1),
     ):
         plan[name] = count
         count += number
@@ -52,11 +52,11 @@
 
 def kernel(
     starts_ref, columns_ref, feat_hbm, ws_hbm, wk_hbm, cot_hbm, tiles_hbm,
-    out_ref, fg_ref, wg_ref,
-    feat_ref, ws_ref, wk_ref, cot_ref, table_v, table,
+    out_hbm, fg_hbm, wg_hbm,
+    out_ref, fg_ref, wg_ref, feat_ref, ws_ref, wk_ref, cot_ref, table_v, table,
     tiles, a_mat, f_buf, p_acc, c_send, c_sib, c_chip, c_recv,
     g_t, r_acc, r_own, r_send, r_sib, r_chip, r_l, r_hs, r_h,
-    w_f32, w_send, w_sib, wy_send, wy_recv, wx_send, wx_recv, wh_all, wl_all, vx_all, vy_all, v_mat,
+    w_f32, w_send, w_sib, wy_send, wy_recv, wx_all, wh_all, wl_all, vy_all, v_mat,
     local_sem, ssem, rsem,
 ):
     loop = lax.axis_index("loop")
@@ -97,6 +97,13 @@
 
     def arrived(landing, name, index, device):
         copy(landing, landing, name, index, device).wait_recv()
+
+    given = []
+
+    def give(src, dst, index):
+        one = pltpu.make_async_copy(src, dst, local_sem.at[9 + index])
+        one.start()
+        given.append(one)
 
     feat_in = pltpu.make_async_copy(feat_hbm, feat_ref, local_sem.at[0])
     others_in = [
@@ -182,16 +189,19 @@
         rows = pl.ds(pl.multiple_of(m * 256, 256), 256)
         return dot(a_mat[4 * j + at, rows, :], f_buf[j, at].reshape(256, FEAT)).reshape(2, TILE, FEAT)
 
-    def add_own(k, first=False):
-        at = turn(h, -k, NH)
-        arrived(f_buf.at[1, at, other], "a_sib", k, sib_dev)
+    def add_own(*turns):
+        places = [turn(h, -k, NH) for k in turns]
+        for k, at in zip(turns, places):
+            arrived(f_buf.at[1, at, other], "a_sib", k, sib_dev)
 
         def step(m, carry):
-            part = product(1, at, m)
-            p_acc[m] = part if first else p_acc[m] + part
+            part = product(1, places[0], m)
+            for at in places[1:]:
+                part = part + product(1, at, m)
+            p_acc[m] = part if turns == (0,) else p_acc[m] + part
             return carry
 
-        lax.fori_loop(0, NH, step, 0)
+        lax.fori_loop(0, NH, step, 0, unroll=True)
 
     def beside_at(k):
         before, after = turn(h_prev, -k, NH), turn(h_next, -k, NH)
@@ -206,15 +216,14 @@
             p_acc[m] = p_acc[m] + (product(0, before, m) + product(2, after, m))
             return carry
 
-        lax.fori_loop(0, NH, step, 0)
+        lax.fori_loop(0, NH, step, 0, unroll=True)
 
     own_in(1)
     own_in(3)
     beside_in(0)
-    add_own(0, first=True)
+    add_own(0)
     own_in(2)
-    add_own(1)
-    add_own(3)
+    add_own(1, 3)
     beside_in(1)
     beside_in(3)
     add_beside(0)
@@ -255,6 +264,7 @@
         send(mine, mine, "e_h", k, h_dev[k])
     send(mine, mine, "e_sib", 0, sib_dev)
     out_ref[...] = (preact * half).astype(BF16)
+    give(out_ref, out_hbm, 0)
 
     w_f32[0] = dot_tn(feat_ref[...], grad_pre)
     w_f32[1] = dot_tn(kernel_rows, grad_pre)
@@ -269,23 +279,32 @@
         rows = pl.ds(pl.multiple_of(at * 256, 256), 256)
         return dot(left, a_mat[n, rows, :])
 
-    def add_back(k, first=False):
-        at = turn(h, -k, NH)
-        arrived(g_t.at[at, other], "e_sib", k, sib_dev)
-        left = gradients(at)
+    def add_back(*turns):
+        places = [turn(h, -k, NH) for k in turns]
+        for k, at in zip(turns, places):
+            arrived(g_t.at[at, other], "e_sib", k, sib_dev)
+        lefts = [gradients(at) for at in places]
 
         def step(n, carry):
-            part = back(at, left, n)
-            r_acc[n] = part if first else r_acc[n] + part
+            part = back(places[0], lefts[0], n)
+            for at, left in zip(places[1:], lefts[1:]):
+                part = part + back(at, left, n)
+            r_acc[n] = part if turns == (0,) else r_acc[n] + part
             return carry
 
-        lax.fori_loop(0, SPAN * NH, step, 0)
+        lax.fori_loop(0, SPAN * NH, step, 0, unroll=True)
 
     def gradient_in(k):
         here = g_t.at[turn(h, -k, NH), core]
         arrived(here, "e_h", k, h_dev[k])
         send(here, here, "e_sib", k, sib_dev)
 
+    def total(parts, count):
+        one = parts[0].astype(F32)
+        for q in range(1, count):
+            one = one + parts[q].astype(F32)
+        return one.astype(BF16)
+
     def chip_rows(block):
         rows = pl.ds(pl.multiple_of(block * 32, 32), 32)
         return w_f32[core, rows, :] + w_sib[rows, :].astype(F32)
@@ -294,97 +313,97 @@
     for k in range(1, NY):
         wy_send[k] = chip_rows(turn(y, k, NY)).astype(BF16)
         send(wy_send.at[k], wy_recv.at[k], "w_y", k, y_dev[k])
-    add_back(0, first=True)
+    add_back(0)
     gradient_in(1)
     gradient_in(3)
     add_back(1)
     gradient_in(2)
+
     for k in range(1, NY):
         arrived(wy_recv.at[k], "w_y", k, y_dev[k])
     part = chip_rows(y)
     for k in range(1, NY):
         part = part + wy_recv[k].astype(F32)
-    for q in range(NX):
-        wx_send[q] = part[(q // 2) * 16:(q // 2 + 1) * 16, (q % 2) * 128:(q % 2 + 1) * 128]
+    wx_all[x] = part.astype(BF16)
     for k in range(1, NX):
-        send(wx_send.at[turn(x, k, NX)], wx_recv.at[k], "w_x", k, x_dev[k])
+        send(wx_all.at[x], wx_all.at[x], "w_x", k, x_dev[k])
 
     add_back(3)
-
-    for k in range(1, NX):
-        arrived(wx_recv.at[k], "w_x", k, x_dev[k])
-    part = wx_send[x]
-    for k in range(1, NX):
-        part = part + wx_recv[k]
-    wh_all[h] = part
-    for k in (2, 1, 3):
-        send(wh_all.at[h], wh_all.at[h], "w_h", k, h_dev[k])
 
     at = turn(h, -2, NH)
     arrived(g_t.at[at, other], "e_sib", 2, sib_dev)
     left = gradients(at)
     first_core = core == 0
 
-    def backward_band(j):
-        for q in range(NH):
-            part = r_acc[4 * j + q] + back(at, left, 4 * j + q)
-            low, high = part[:, :TILE], part[:, TILE:]
-            r_send[j, q] = jnp.where(first_core, high, low).astype(BF16)
-            send(r_send.at[j, q], r_sib.at[j, q], "g_sib", 4 * j + q, sib_dev)
-            r_own[j, q] = jnp.where(first_core, low, high)
-
-    def to_beside(j, device):
-        for q in range(NH):
-            arrived(r_sib.at[j, q], "g_sib", 4 * j + q, sib_dev)
-            r_chip[j // 2, q] = (r_own[j, q] + r_sib[j, q].astype(F32)).astype(BF16)
-            send(r_chip.at[j // 2, q], r_l.at[j // 2, q], "g_l", 2 * j + q, device)
-
-    backward_band(0)
-    backward_band(2)
-    to_beside(0, prev_dev)
-    to_beside(2, next_dev)
-
-    backward_band(1)
+    def products_back(j, base, k):
+        q = turn(base, k, NH)
+        part = r_acc[4 * j + q] + back(at, left, 4 * j + q)
+        low, high = part[:, :TILE], part[:, TILE:]
+        r_send[j, k] = jnp.where(first_core, high, low).astype(BF16)
+        send(r_send.at[j, k], r_sib.at[j, k], "g_sib", 4 * j + k, sib_dev)
+        r_own[j, k] = jnp.where(first_core, low, high)
+
+    def to_beside(j, k, device):
+        arrived(r_sib.at[j, k], "g_sib", 4 * j + k, sib_dev)
+        r_chip[j // 2, k] = (r_own[j, k] + r_sib[j, k].astype(F32)).astype(BF16)
+        send(r_chip.at[j // 2, k], r_l.at[j // 2, k], "g_l", 2 * j + k, device)
+
+    def summed(k):
+        arrived(r_sib.at[1, k], "g_sib", 4 + k, sib_dev)
+        arrived(r_l.at[0, k], "g_l", k, next_dev)
+        arrived(r_l.at[1, k], "g_l", 4 + k, prev_dev)
+        return (r_own[1, k] + r_sib[1, k].astype(F32)) + (r_l[0, k].astype(F32) + r_l[1, k].astype(F32))
+
+    def to_holder(k):
+        r_hs[k] = summed(k).astype(BF16)
+        send(r_hs.at[k], r_h.at[k], "g_h", k, h_dev[k])
+
+    order = (2, 1, 3, 0)
+    for step, k in enumerate(order):
+        products_back(0, h_prev, k)
+        products_back(2, h_next, k)
+        if step > 0:
+            to_beside(0, order[step - 1], prev_dev)
+            to_beside(2, order[step - 1], next_dev)
+        if step == 1:
+            for q in range(1, NX):
+                arrived(wx_all.at[turn(x, -q, NX)], "w_x", q, x_dev[q])
+            wh_all[h] = total(wx_all, NX)
+            for q in (2, 1, 3):
+                send(wh_all.at[h], wh_all.at[h], "w_h", q, h_dev[q])
+    products_back(1, h, 2)
+    to_beside(0, 0, prev_dev)
+    to_beside(2, 0, next_dev)
+    for k in (1, 3, 0):
+        products_back(1, h, k)
 
     for k in range(1, NH):
         arrived(wh_all.at[turn(h, -k, NH)], "w_h", k, h_dev[k])
-    wl_all[l] = (wh_all[0] + wh_all[1]) + (wh_all[2] + wh_all[3])
+    wl_all[l] = total(wh_all, NH)
     for k in range(1, NL):
         send(wl_all.at[l], wl_all.at[l], "w_l", k, l_dev[k])
 
-    for q in range(NH):
-        arrived(r_sib.at[1, q], "g_sib", 4 + q, sib_dev)
-    r_own[1] = r_own[1] + r_sib[1].astype(F32)
+    to_holder(2)
 
     for k in range(1, NL):
         arrived(wl_all.at[turn(l, -k, NL)], "w_l", k, l_dev[k])
-    vx_all[x] = (wl_all[0] + wl_all[1] + wl_all[2]).astype(BF16)
-    for k in range(1, NX):
-        send(vx_all.at[x], vx_all.at[x], "v_x", k, x_dev[k])
-    for q in range(NH):
-        arrived(r_l.at[0, q], "g_l", q, next_dev)
-        arrived(r_l.at[1, q], "g_l", 4 + q, prev_dev)
-
-    def summed(block):
-        return r_own[1, block] + (r_l[0, block].astype(F32) + r_l[1, block].astype(F32))
-
-    for k in (2, 1, 3):
-        r_hs[k] = summed(turn(h, k, NH)).astype(BF16)
-        send(r_hs.at[k], r_h.at[k], "g_h", k, h_dev[k])
-    returned = returned + summed(h)
-
-    for k in range(1, NX):
-        arrived(vx_all.at[turn(x, -k, NX)], "v_x", k, x_dev[k])
-    vy_all[y] = jnp.concatenate(
-        [jnp.concatenate([vx_all[2 * q], vx_all[2 * q + 1]], axis=1) for q in range(NX // 2)], axis=0
-    )
+    vy_all[y] = total(wl_all, NL)
     for k in range(1, NY):
         send(vy_all.at[y], vy_all.at[y], "v_y", k, y_dev[k])
+
+    to_holder(1)
+    to_holder(3)
+    returned = returned + summed(0)
+
+    settled = len(started) - 2 * NY
+    for one in started[:settled]:
+        one.wait_send()
 
     for k in (1, 3, 2):
         arrived(r_h.at[k], "g_h", k, h_dev[k])
         returned = returned + r_h[k].astype(F32)
     fg_ref[...] = returned.T.astype(BF16)
+    give(fg_ref, fg_hbm, 1)
 
     for k in range(1, NY):
         arrived(vy_all.at[turn(y, -k, NY)], "v_y", k, y_dev[k])
@@ -392,15 +411,22 @@
     send(v_mat.at[core], v_mat.at[core], "v_sib", 0, sib_dev)
     scale = 1.0 / math.sqrt(TILE * REPS * BANDS)
     wg_ref[core] = v_mat[core].astype(F32) * scale
+    give(wg_ref.at[core], wg_hbm.at[core], 2)
     arrived(v_mat.at[other], "v_sib", 0, sib_dev)
     wg_ref[other] = v_mat[other].astype(F32) * scale
-
-    for one in started:
+    give(wg_ref.at[other], wg_hbm.at[other], 3)
+
+    for one in started[settled:]:
         one.wait_send()
+    for one in given:
+        one.wait()
 
 
 def scratch():
     return [
+        pltpu.VMEM((TILE, FEAT), BF16),
+        pltpu.VMEM((TILE, FEAT), BF16),
+        pltpu.VMEM((2, FEAT, FEAT), F32),
         pltpu.VMEM((TILE, FEAT), BF16),
         pltpu.VMEM((FEAT, FEAT), BF16),
         pltpu.VMEM((FEAT, FEAT), BF16),
@@ -429,14 +455,12 @@
         pltpu.VMEM((FEAT, FEAT), BF16),
         pltpu.VMEM((NY, 32, FEAT), BF16),
         pltpu.VMEM((NY, 32, FEAT), BF16),
-        pltpu.VMEM((NX, 16, 128), F32),
-        pltpu.VMEM((NX, 16, 128), F32),
-        pltpu.VMEM((NH, 16, 128), F32),
-        pltpu.VMEM((NL, 16, 128), F32),
-        pltpu.VMEM((NX, 16, 128), BF16),
+        pltpu.VMEM((NX, 32, FEAT), BF16),
+        pltpu.VMEM((NH, 32, FEAT), BF16),
+        pltpu.VMEM((NL, 32, FEAT), BF16),
         pltpu.VMEM((NY, 32, FEAT), BF16),
         pltpu.VMEM((2, FEAT, FEAT), BF16),
-        pltpu.SemaphoreType.DMA((9,)),
+        pltpu.SemaphoreType.DMA((13,)),
         pltpu.SemaphoreType.DMA((N_SEMS,)),
         pltpu.SemaphoreType.DMA((N_SEMS,)),
     ]
@@ -467,7 +491,7 @@
         kernel,
         out_shape=shapes,
         in_specs=[pl.BlockSpec(memory_space=pltpu.SMEM), vmem, hbm, hbm, hbm, hbm, hbm],
-        out_specs=(vmem, vmem, vmem),
+        out_specs=(pl.BlockSpec(memory_space=pl.ANY),) * 3,
         scratch_shapes=scratch(),
         compiler_params=pltpu.CompilerParams(
             collective_id=0, has_side_effects=True, vmem_limit_bytes=64 * 1024 * 1024 - 65536

time: 98.9 us -> 91.6 us (0.926)
  Pallas kernels: 97.2 us -> 90.4 us
    pallas_call x1, Pallas kernels: 95.2 us -> 88.4 us  [on_device(): pl.pallas_call(kernel, out_shape=shapes, in_specs=[pl.BlockSpec(memory_sp...]
where the time goes in v3:
time: 91.6 us; the launch traced here: 91 us
  Pallas kernels  90.4 us (99%)
    pallas_call x1, Pallas kernels, on_device(): pl.pallas_call(kernel, out_shape=shapes, in_specs=[pl.BlockSpec(memory_sp...  88.4 us
    pallas_call x1, Pallas kernels, on_device(): pl.pallas_call(hand_out, out_shape=shapes, in_specs=[pl.BlockSpec(memory_...  1.97 us

profile of v3, /device:TPU:1, one launch (start us, length us, event | category | flops | bytes accessed | tf_op | source)
XLA Modules:
  0.0 91.0 jit_solution(13583272870679119415)
XLA Ops:
  0.6 88.4 %shard_map.94 = (bf16[128,256]{1,0:T(8,128)(2,1)}, bf16[128,256]{1,0:T(8,128)(2,1)}, f32[2,256,256]{2,1,0:T(8,128)}) custom-call(s32[1,9]{1,0:T(1,128)} %starts_ref.1, s32[1,128]{1,0:T(1,128)} %columns_ref.1, bf16[128,256]{1,0:T(8,128)(2,1)} %feat_hbm.1, bf16[256,256]{1,0:T(8,128)(2,1)} %ws_hbm.1, bf16[256,256]{1,0:T(8,128)(2,1)} %wk_hbm.1, ...), custom_call_target="tpu_custom_call" | custom-call | tf_op jit(solution)/shard_map/pallas_call | solution.py:490
  89.1 2.0 %shard_map.95 = (bf16[128,256]{1,0:T(8,128)(2,1)}, bf16[128,256]{1,0:T(8,128)(2,1)}, f32[2,256,256]{2,1,0:T(8,128)}) custom-call(bf16[128,256]{1,0:T(8,128)(2,1)} %get-tuple-element.6.refs_0_, bf16[128,256]{1,0:T(8,128)(2,1)} %get-tuple-element.7.refs_1_, f32[2,256,256]{2,1,0:T(8,128)} %get-tuple-element.8.refs_2_), custom_call_target="tpu_custom_call" | custom-call | tf_op jit(solution)/shard_map/pallas_call | solution.py:500

commit v4 on v3

--- a/solution.py
+++ b/solution.py
@@ -218,6 +218,7 @@
 
         lax.fori_loop(0, NH, step, 0, unroll=True)
 
+    self_part = dot(feat_ref[...], ws_ref[...])
     own_in(1)
     own_in(3)
     beside_in(0)
@@ -229,7 +230,6 @@
     add_beside(0)
     add_own(2)
     add_beside(1)
-    self_part = dot(feat_ref[...], ws_ref[...])
     beside_in(2)
     add_beside(3)
 
@@ -365,15 +365,14 @@
         if step > 0:
             to_beside(0, order[step - 1], prev_dev)
             to_beside(2, order[step - 1], next_dev)
-        if step == 1:
-            for q in range(1, NX):
-                arrived(wx_all.at[turn(x, -q, NX)], "w_x", q, x_dev[q])
-            wh_all[h] = total(wx_all, NX)
-            for q in (2, 1, 3):
-                send(wh_all.at[h], wh_all.at[h], "w_h", q, h_dev[q])
     products_back(1, h, 2)
     to_beside(0, 0, prev_dev)
     to_beside(2, 0, next_dev)
+    for q in range(1, NX):
+        arrived(wx_all.at[turn(x, -q, NX)], "w_x", q, x_dev[q])
+    wh_all[h] = total(wx_all, NX)
+    for q in (2, 1, 3):
+        send(wh_all.at[h], wh_all.at[h], "w_h", q, h_dev[q])
     for k in (1, 3, 0):
         products_back(1, h, k)
 

time: 91.6 us -> 97.5 us (1.064)
  the two profiles are of different devices: /device:TPU:1 before, /device:TPU:11 now
where the time goes in v4:
time: 97.5 us; the launch traced here: 97.3 us
  Pallas kernels  96.7 us (99%)
    pallas_call x1, Pallas kernels, on_device(): pl.pallas_call(kernel, out_shape=shapes, in_specs=[pl.BlockSpec(memory_sp...  94.7 us
    pallas_call x1, Pallas kernels, on_device(): pl.pallas_call(hand_out, out_shape=shapes, in_specs=[pl.BlockSpec(memory_...  1.97 us

profile of v4, /device:TPU:11, one launch (start us, length us, event | category | flops | bytes accessed | tf_op | source)
XLA Modules:
  0.0 97.3 jit_solution(5958852423231344150)
XLA Ops:
  0.6 94.7 %shard_map.94 = (bf16[128,256]{1,0:T(8,128)(2,1)}, bf16[128,256]{1,0:T(8,128)(2,1)}, f32[2,256,256]{2,1,0:T(8,128)}) custom-call(s32[1,9]{1,0:T(1,128)} %starts_ref.1, s32[1,128]{1,0:T(1,128)} %columns_ref.1, bf16[128,256]{1,0:T(8,128)(2,1)} %feat_hbm.1, bf16[256,256]{1,0:T(8,128)(2,1)} %ws_hbm.1, bf16[256,256]{1,0:T(8,128)(2,1)} %wk_hbm.1, ...), custom_call_target="tpu_custom_call" | custom-call | tf_op jit(solution)/shard_map/pallas_call | solution.py:489
  95.4 2.0 %shard_map.95 = (bf16[128,256]{1,0:T(8,128)(2,1)}, bf16[128,256]{1,0:T(8,128)(2,1)}, f32[2,256,256]{2,1,0:T(8,128)}) custom-call(bf16[128,256]{1,0:T(8,128)(2,1)} %get-tuple-element.6.refs_0_, bf16[128,256]{1,0:T(8,128)(2,1)} %get-tuple-element.7.refs_1_, f32[2,256,256]{2,1,0:T(8,128)} %get-tuple-element.8.refs_2_), custom_call_target="tpu_custom_call" | custom-call | tf_op jit(solution)/shard_map/pallas_call | solution.py:499
